TPU v7x, 128 devices: a whole 4x4x4 slice. The times are simulated.
128 devices in a mesh: col: 8 (over y_lo, x), dev: 8 (over y_hi, z), ao: 2 (over core).
Axes of the slice: x: 4, y: 4 (y_hi: 2, y_lo: 2; y = y_hi * 2 + y_lo), z: 4, core: 2. Of those that a mesh axis runs over, the one named last changes fastest.
Arguments:
- raw_ints: bfloat16 [1024, 32, 512], P('dev', None, 'col'), may hold values from -1.078125 to 1.078125
- metric: bfloat16 [1024, 1024], P('dev'), may hold values from -0.1875 to 0.1875
- amplitudes: bfloat16 [512, 512, 2048], P('col', 'dev', 'ao'), may hold values from -0.017944336 to 0.017944336
- pair_list: int32 [2, 2048], P(None, 'ao'), may hold values from 0 to 63
- occ_energy: float32 [64], replicated, may hold values from -2 to -0.3
- vir_energy: float32 [512], replicated, may hold values from 0.2 to 3
- window_ids: int32 [32], replicated, may hold values from 0 to 511, as said below
Outputs:
- residual: float32 [1024, 2048], P(('col', 'dev'), 'ao')
Inputs may be any that keep to these rules, and one draw needn't show every extreme that they name: `window_ids`: distinct virtual orbitals; 0 and 511 are always among them.
All inputs are finite; a program needn't handle non-finite values.
Results may differ from a plain program's by a relative error of at most 0.0041.
Values may be sent and summed in bfloat16 or wider, within the bound.
A program may use at most 128 MiB of HBM per device.

v0:
```python
import jax
import jax.numpy as jnp
from jax import lax
from jax.sharding import PartitionSpec as P


def select_energy(positions, table):
    labels = jnp.arange(table.shape[0], dtype=jnp.int32)
    return jnp.sum(jnp.where(positions[:, None] == labels[None, :], table[None, :], 0.0), axis=1)


def on_device(raw_ints, metric, amplitudes, pair_list, occ_energy, vir_energy, window_ids):
    full_width = raw_ints.shape[1]
    local_aux = metric.shape[0]
    rows_used = raw_ints.shape[1]
    c_block = raw_ints.shape[2]
    raw_block = lax.all_gather(raw_ints, "dev", axis=0, tiled=True)
    row_count = raw_block.shape[0]
    transformed = jnp.dot(
        metric,
        raw_block.reshape(row_count, rows_used * c_block),
        preferred_element_type=jnp.float32,
    )
    transformed = transformed.astype(jnp.bfloat16).reshape(local_aux, rows_used, c_block)
    spread = lax.all_gather(transformed, "col", axis=2, tiled=True)
    right_factor = lax.all_to_all(spread, "dev", split_axis=2, concat_axis=0, tiled=True)
    d_block = right_factor.shape[2]
    contract = (((0,), (0,)), ((), ()))
    left_block = lax.all_gather(transformed, "dev", axis=0, tiled=True)
    row_count = left_block.shape[0]
    integrals = lax.dot_general(
        left_block.reshape(row_count, full_width * c_block),
        right_factor.reshape(row_count, full_width * d_block),
        contract,
        preferred_element_type=jnp.float32,
    )
    ladder_flat = integrals.astype(jnp.bfloat16)
    ladder = ladder_flat.reshape(full_width, c_block, full_width, d_block)
    ladder = jnp.transpose(ladder, (0, 2, 1, 3)).reshape(full_width * full_width, c_block * d_block)
    partial_value = jnp.dot(
        ladder,
        amplitudes.reshape(c_block * d_block, amplitudes.shape[2]),
        preferred_element_type=jnp.float32,
    )
    summed = lax.psum_scatter(partial_value, ("col", "dev"), scatter_dimension=0, tiled=True)
    row_total = summed.shape[0]
    global_rows = lax.axis_index(("col", "dev")) * row_total + jnp.arange(
        row_total, dtype=jnp.int32
    )
    window_energy = select_energy(window_ids, vir_energy)
    energy_first = select_energy(global_rows // full_width, window_energy)
    energy_second = select_energy(global_rows % full_width, window_energy)
    energy_i = select_energy(pair_list[0], occ_energy)
    energy_j = select_energy(pair_list[1], occ_energy)
    denominator = (energy_i + energy_j)[None, :] - (energy_first + energy_second)[:, None]
    return summed / denominator


def solution(mesh):
    in_specs = (
        P("dev", None, "col"),
        P("dev", None),
        P("col", "dev", "ao"),
        P(None, "ao"),
        P(),
        P(),
        P(),
    )
    out_specs = P(("col", "dev"), "ao")
    return jax.shard_map(
        on_device, mesh=mesh, in_specs=in_specs, out_specs=out_specs, check_vma=False
    )
```

profile of v0, /device:TPU:0, one launch (start us, length us, event | category | flops | bytes accessed | tf_op | source)
XLA Modules:
  0.0 704.8 jit_solution(10385074896995963126)
XLA Ops:
  6.5 0.7 all-gather.4.cloned.1.call-update
  7.3 0.0 all-gather.8.cloned.1.call-start
  7.3 78.6 %all-gather.4.cloned.1.call-done = bf16[1024,32,64]{0,2,1:T(8,128)(2,1)} async-done(((bf16[128,32,64]{0,2,1:T(8,128)(2,1)}), bf16[1024,32,64]{0,2,1:T(8,128)(2,1)}) %all-gather.4.cloned.1.call-update) | async-done | bytes 4194320 | tf_op jit(solution)/shard_map/all_gather | solution.py:17
  85.9 3.7 convolution_convert_fusion.1
  89.6 1.1 copy.16
  90.7 0.0 all-gather.6.cloned.1.call-start
  90.7 0.7 all-gather.6.cloned.1.call-update
  91.4 0.0 reduce-scatter.2.cloned.1.call-start
  91.5 49.7 %all-gather.8.cloned.1.call-done = bf16[128,32,512]{0,2,1:T(8,128)(2,1)} async-done(((bf16[128,32,64]{0,2,1:T(8,128)(2,1)}), bf16[128,32,512]{0,2,1:T(8,128)(2,1)}) %all-gather.8.cloned.1.call-update) | async-done | bytes 4194320 | tf_op jit(solution)/shard_map/all_gather | solution.py:25
  141.1 4.9 copy.17
  146.0 63.3 %all_to_all.15 = bf16[128,32,512]{0,1,2:T(8,128)(2,1)S(1)} all-to-all(bf16[128,32,512]{0,1,2:T(8,128)(2,1)S(1)} %copy.17), channel_id=1, replica_groups=mesh['col'=8,'dev'=8,'ao'=2] {'dev'}, dimensions={2} | all-to-all | bytes 8388608 | tf_op jit(solution)/shard_map/all_to_all | solution.py:26
  209.3 4.7 copy.19
  214.0 33.4 %all-gather.6.cloned.1.call-done = bf16[1024,32,64]{0,2,1:T(8,128)(2,1)} async-done(((bf16[128,32,64]{0,2,1:T(8,128)(2,1)}), bf16[1024,32,64]{0,2,1:T(8,128)(2,1)}) %all-gather.6.cloned.1.call-update) | async-done | bytes 4194320 | tf_op jit(solution)/shard_map/all_gather | solution.py:29
  247.4 14.0 %convolution_convert_fusion = bf16[2048,2048]{1,0:T(8,128)(2,1)} fusion(bf16[1024,2048]{0,1:T(8,128)(2,1)} %bitcast.35, bf16[256,8,8,128]{3,2,1,0:T(8,128)(2,1)} %bitcast.31), kind=kOutput, calls=%fused_computation.1 | convolution fusion | flops 8594128896 | bytes 16777216 | tf_op jit(solution)/shard_map/dot_general | solution.py:31
  261.4 24.4 %reshape.74 = bf16[32,64,32,64]{3,2,1,0:T(8,128)(2,1)} reshape(bf16[2048,2048]{1,0:T(8,128)(2,1)} %convolution_convert_fusion) | data formatting | bytes 16777216 | tf_op jit(solution)/shard_map/reshape | solution.py:38
  285.8 17.5 %copy.28 = bf16[32,64,32,64]{3,1,2,0:T(8,128)(2,1)} copy(bf16[32,64,32,64]{3,2,1,0:T(8,128)(2,1)} %reshape.74) | data formatting | bytes 16777216 | tf_op jit(solution)/shard_map/reshape | solution.py:38
  303.3 22.6 %reshape.75 = bf16[1024,4096]{1,0:T(8,128)(2,1)} reshape(bf16[32,32,64,64]{3,2,1,0:T(8,128)(2,1)} %bitcast.26) | data formatting | bytes 16777216 | tf_op jit(solution)/shard_map/reshape | solution.py:39
  325.9 15.1 %fusion.3 = f32[1024,1024]{1,0:T(8,128)} fusion(bf16[1024,4096]{1,0:T(8,128)(2,1)} %reshape.75, bf16[4096,1024]{1,0:T(8,128)(2,1)} %bitcast.34), kind=kOutput, calls=%fused_computation.23 | convolution fusion | flops 8589934592 | bytes 20971520 | tf_op jit(solution)/shard_map/dot_general | solution.py:40
  341.1 0.6 copy-done.3
  341.7 0.2 select_reduce_fusion.2
  341.9 0.2 select_reduce_fusion.3
  342.1 0.2 select_reduce_fusion
  342.3 354.4 %reduce-scatter.2.cloned.1.call-done = f32[16,1024]{1,0:T(8,128)} async-done(((f32[1024,1024]{1,0:T(8,128)}), f32[16,1024]{1,0:T(8,128)}) %reduce-scatter.2.cloned.1.call-update) | async-done | bytes 65552 | tf_op jit(solution)/shard_map/reduce_scatter | solution.py:45
  696.7 1.6 subtract_divide_fusion
  (18 shorter events, 0.1 us)
Async XLA Ops:
  6.5 79.4 %copy-start = (bf16[128,1024]{1,0:T(8,128)(2,1)S(1)}, bf16[128,1024]{1,0:T(8,128)(2,1)}, u32[]{:S(2)}) copy-start(bf16[128,1024]{1,0:T(8,128)(2,1)} %param.8) | copy-start | bytes 786436
  6.5 79.4 %all-gather.4.cloned.1.call-start = ((), (), s32[]{:S(2)}) async-start(), calls=%async_computation.2 | async-start | bytes 4718592 | tf_op jit(solution)/shard_map/all_gather | solution.py:17
  7.3 133.9 %all-gather.8.cloned.1.call-start = ((), (), s32[]{:S(2)}) async-start(), calls=%async_computation.4 | async-start | bytes 4718592 | tf_op jit(solution)/shard_map/all_gather | solution.py:25
  90.7 156.7 %all-gather.6.cloned.1.call-start = ((), (), s32[]{:S(2)}) async-start(), calls=%async_computation.3 | async-start | bytes 4718592 | tf_op jit(solution)/shard_map/all_gather | solution.py:29
  91.4 605.3 %reduce-scatter.2.cloned.1.call-start = ((), (), s32[]{:S(2)}) async-start(), calls=%async_computation.5 | async-start | bytes 4259840 | tf_op jit(solution)/shard_map/reduce_scatter | solution.py:45
  325.9 372.3 %copy-start.1 = (bf16[128,1024]{1,0:T(8,128)(2,1)S(1)}, bf16[128,1024]{1,0:T(8,128)(2,1)}, u32[]{:S(2)}) copy-start(bf16[128,1024]{1,0:T(8,128)(2,1)} %param.8) | copy-start | bytes 786436
  341.0 0.7 copy-start.3
  341.0 0.7 copy-start.5
  341.0 1.1 copy-start.2
  341.0 1.1 copy-start.4
Sparse Core Ops, SparseCore 0:
  9.5 76.3 all-gather.3
  90.8 50.3 all-gather.7
  143.3 104.0 all-gather.5
  341.2 355.4 reduce-scatter.1
where the time goes:
time: 706 us; the launch traced here: 705 us
  waiting for transfers between devices  517 us (73%)
  local copies, waits for them, and re-layouts  75.7 us (11%)
  blocking collectives  63.3 us (9%)
  matrix products  32.8 us (5%)
  between operations  13.2 us (2%)
    reduce_scatter x1, waiting for transfers between devices, on_device(): lax.psum_scatter(partial_value, ('col', 'dev'), scatter_dimension=0, tile...  354 us
    all_gather x1, waiting for transfers between devices, on_device(): raw_block = lax.all_gather(raw_ints, 'dev', axis=0, tiled=True)  78.6 us
    all_to_all x1, blocking collectives, on_device(): lax.all_to_all(spread, 'dev', split_axis=2, concat_axis=0, tiled=True)  63.3 us
    all_gather x1, waiting for transfers between devices, on_device(): spread = lax.all_gather(transformed, 'col', axis=2, tiled=True)  49.7 us
    reshape x2, local copies, waits for them, and re-layouts, on_device(): ladder = ladder_flat.reshape(full_width, c_block, full_width, d_block)  41.9 us
    all_gather x1, waiting for transfers between devices, on_device(): left_block = lax.all_gather(transformed, 'dev', axis=0, tiled=True)  33.4 us
    reshape x1, local copies, waits for them, and re-layouts, on_device(): jnp.transpose(ladder, (0, 2, 1, 3))  22.6 us
    dot_general x1, matrix products, on_device(): jnp.dot(ladder, amplitudes.reshape(c_block * d_block, amplitudes.shape[2]...  15.1 us
  transfers between devices with their start and end apart: 4, of which 4 were waited for; matrix products, arithmetic and copies ran while one was open for 1% of the time, Pallas kernels for 0%

commit v1 on v0

v1 whole, which is shorter than its diff:
```python
import jax
import jax.numpy as jnp
from jax import lax
from jax.experimental import pallas as pl
from jax.experimental.pallas import tpu as pltpu
from jax.sharding import PartitionSpec as P

MESH = pl.DeviceIdType.MESH
F32, BF16 = jnp.float32, jnp.bfloat16
NT = (((1,), (1,)), ((), ()))

PARTNER, MINUS, PLUS, MINUS_P, PLUS_P, FAR_A, FAR_AP, FAR_B, FAR_BP = range(9)
SWAP = 9


def select_energy(positions, table):
    labels = jnp.arange(table.shape[0], dtype=jnp.int32)
    return jnp.sum(jnp.where(positions[:, None] == labels[None, :], table[None, :], 0.0), axis=1)


def ladder_kernel(
    raw_ca, raw_bd, met, amp, out,
    work, mbuf, acc_l, acc_r, fac_l, fac_r, amps, sums, send1, land1, send2, land2,
    local_sem, ag_send, ag_recv, rel_send, rel_recv, rs_send, rs_recv,
):
    i, j, o = lax.axis_index("col"), lax.axis_index("dev"), lax.axis_index("ao")
    flip = lambda g: lax.rem(g + 4, 8)
    ring = lambda g, step: (g // 4) * 4 + lax.rem(lax.rem(g, 4) + step, 4)
    along_dev = lambda g: (i, g, o)
    along_col = lambda g: (g, j, o)
    sibling = (i, j, 1 - o)
    swap = (j, i, o)

    barrier = pltpu.get_barrier_semaphore()

    def greet(device):
        pl.semaphore_signal(barrier, inc=1, device_id=device, device_id_type=MESH)

    for d in range(1, 8):
        greet(along_dev(lax.rem(j + d, 8)))
        greet(along_col(lax.rem(i + d, 8)))
    greet(sibling)
    greet((flip(i), flip(j), o))

    @pl.when(i != j)
    def _():
        greet(swap)

    pl.semaphore_wait(barrier, 16 + jnp.where(i != j, 1, 0))

    pending = []

    def push(src, dst, send_sem, recv_sem, device):
        copy = pltpu.make_async_remote_copy(
            src_ref=src, dst_ref=dst, send_sem=send_sem, recv_sem=recv_sem,
            device_id=device, device_id_type=MESH,
        )
        copy.start()
        pending.append(copy)

    def landed(dst, recv_sem):
        pltpu.make_async_remote_copy(
            src_ref=dst, dst_ref=dst, send_sem=recv_sem, recv_sem=recv_sem,
            device_id=sibling, device_id_type=MESH,
        ).wait_recv()

    class Gather:
        def __init__(self, which, me, to, partner, half, part):
            self.which, self.me, self.half, self.part = which, me, half, part
            self.up, self.down = to(ring(me, 1)), to(ring(me, 3))
            self.partner = partner
            plus, minus, far = ring(me, 1), ring(me, 3), ring(me, 2)
            self.plus, self.minus, self.far = plus, minus, far
            self.place = {
                PARTNER: (flip(me), None), MINUS: (minus, None), PLUS: (plus, None),
                MINUS_P: (flip(minus), None), PLUS_P: (flip(plus), None),
                FAR_A: (far, 0), FAR_AP: (flip(far), 0), FAR_B: (far, 1), FAR_BP: (flip(far), 1),
            }

        def spot(self, kind, core):
            piece, quarter = self.place[kind]
            if quarter is None:
                return self.half(piece, core)
            return self.part(piece, core, quarter)

        def send(self, src, dst, kind, device):
            push(src, dst, ag_send.at[self.which, kind], ag_recv.at[self.which, kind], device)

        def send_own(self, src):
            dst = self.half(self.me, o)
            self.send(src, dst, MINUS, self.up)
            self.send(src, dst, PLUS, self.down)
            self.send(src, dst, PARTNER, self.partner)

        def arrive(self, *kinds):
            for kind in kinds:
                spot = self.spot(kind, o)
                landed(spot, ag_recv.at[self.which, kind])
                if kind == PARTNER:
                    self.send(spot, spot, MINUS_P, self.up)
                    self.send(spot, spot, PLUS_P, self.down)
                elif kind in (MINUS, MINUS_P):
                    piece = self.part(self.place[kind][0], o, 0)
                    self.send(piece, piece, FAR_A if kind == MINUS else FAR_AP, self.up)
                elif kind in (PLUS, PLUS_P):
                    piece = self.part(self.place[kind][0], o, 1)
                    self.send(piece, piece, FAR_B if kind == PLUS else FAR_BP, self.down)
                push(spot, spot, rel_send.at[self.which, kind], rel_recv.at[self.which, kind], sibling)

        def from_sibling(self, *kinds):
            for kind in kinds:
                landed(self.spot(kind, 1 - o), rel_recv.at[self.which, kind])

    left = Gather(
        0, j, along_dev, along_dev(flip(j)),
        lambda k, core: work.at[2 * k + core],
        lambda k, core, q: work.at[2 * k + core, pl.ds(512 * q, 512)],
    )
    right = Gather(
        1, i, along_col, along_col(flip(i)),
        lambda k, core: work.at[16 + 2 * k + core],
        lambda k, core, q: work.at[16 + 2 * k + core, pl.ds(512 * q, 512)],
    )
    fit = Gather(
        2, j, along_dev, (flip(i), flip(j), o),
        lambda k, core: mbuf.at[k, pl.ds(pl.multiple_of(64 * core, 64), 64)],
        lambda k, core, q: mbuf.at[k, pl.ds(pl.multiple_of(64 * core + 32 * q, 32), 32)],
    )

    own_half = pl.ds(pl.multiple_of(1024 * o, 1024), 1024)
    swap_dst = work.at[16 + 2 * j + o]
    swap_src = raw_bd.at[own_half]
    swap_here = work.at[16 + 2 * i + o]

    fit.send_own(met.at[pl.ds(pl.multiple_of(64 * o, 64), 64)])
    left.send_own(raw_ca.at[own_half])
    swap_copy = pltpu.make_async_remote_copy(
        src_ref=swap_src, dst_ref=swap_dst, send_sem=ag_send.at[1, SWAP],
        recv_sem=ag_recv.at[1, SWAP], device_id=swap, device_id_type=MESH,
    )

    @pl.when(i != j)
    def _():
        swap_copy.start()

    @pl.when(i == j)
    def _():
        here = pltpu.make_async_copy(swap_src, swap_here, local_sem.at[3])
        here.start()
        here.wait()

    own_l = [
        pltpu.make_async_copy(raw_ca.at[pl.ds(1024 * h, 1024)], work.at[2 * j + h], local_sem.at[4 + h])
        for h in range(2)
    ]
    own_m = pltpu.make_async_copy(met, mbuf.at[j], local_sem.at[1])
    get_amps = pltpu.make_async_copy(amp, amps, local_sem.at[2])
    for copy in own_l + [own_m, get_amps]:
        copy.start()

    fit.arrive(PARTNER)
    left.arrive(PARTNER)

    @pl.when(i != j)
    def _():
        landed(swap_here, ag_recv.at[1, SWAP])

    right.send_own(swap_here)
    push(swap_here, swap_here, rel_send.at[1, SWAP], rel_recv.at[1, SWAP], sibling)
    fit.arrive(MINUS, PLUS, MINUS_P, PLUS_P)
    left.arrive(MINUS, PLUS)
    right.arrive(PARTNER)
    left.arrive(MINUS_P, PLUS_P)
    fit.arrive(FAR_A, FAR_B, FAR_AP, FAR_BP)
    for copy in own_l + [own_m]:
        copy.wait()
    fit.from_sibling(*range(9))

    def m_slice(k):
        return mbuf[:, :, pl.ds(pl.multiple_of(k * 128, 128), 128)].reshape(1024, 128)

    def fit_left(k, first=False, last=False):
        two = flip(k)
        m = jnp.concatenate([m_slice(k), m_slice(two)], axis=1)

        def body(n, _):
            h, at = n // 2, pl.multiple_of(lax.rem(n, 2) * 512, 512)
            rows = pl.ds(pl.multiple_of(n * 512, 512), 512)
            x = jnp.concatenate([work[2 * k + h, pl.ds(at, 512), :], work[2 * two + h, pl.ds(at, 512), :]], axis=1)
            y = lax.dot_general(x, m, NT, preferred_element_type=F32)
            if not first:
                y = y + acc_l[rows, :]
            if last:
                fac_l[rows, :] = y.astype(BF16)
            else:
                acc_l[rows, :] = y
            return 0

        lax.fori_loop(0, 4, body, 0)

    def fit_right(k, first=False, last=False):
        two = flip(k)
        m = jnp.concatenate([m_slice(k), m_slice(two)], axis=1)

        def body(n, _):
            h, at = n // 2, pl.multiple_of(lax.rem(n, 2) * 512, 512)
            cols = pl.ds(pl.multiple_of(n * 512, 512), 512)
            x = jnp.concatenate(
                [work[16 + 2 * k + h, pl.ds(at, 512), :], work[16 + 2 * two + h, pl.ds(at, 512), :]], axis=1)
            y = lax.dot_general(m, x, NT, preferred_element_type=F32)
            if not first:
                y = y + acc_r[:, cols]
            if last:
                fac_r[:, cols] = y.astype(BF16)
            else:
                acc_r[:, cols] = y
            return 0

        lax.fori_loop(0, 4, body, 0)

    left.from_sibling(PARTNER)
    fit_left(left.me, first=True)
    right.arrive(MINUS, PLUS)
    left.from_sibling(MINUS, MINUS_P)
    fit_left(left.minus)
    right.arrive(MINUS_P, PLUS_P)
    left.from_sibling(PLUS, PLUS_P)
    fit_left(left.plus)
    left.arrive(FAR_A, FAR_B, FAR_AP, FAR_BP)
    landed(work.at[16 + 2 * i + 1 - o], rel_recv.at[1, SWAP])
    right.from_sibling(PARTNER)
    fit_right(right.me, first=True)
    right.from_sibling(MINUS, MINUS_P)
    fit_right(right.minus)
    right.from_sibling(PLUS, PLUS_P)
    fit_right(right.plus)
    left.from_sibling(FAR_A, FAR_B, FAR_AP, FAR_BP)
    fit_left(left.far, last=True)
    right.arrive(FAR_A, FAR_B, FAR_AP, FAR_BP)
    right.from_sibling(FAR_A, FAR_B, FAR_AP, FAR_BP)
    fit_right(right.far, last=True)

    for copy in pending:
        copy.wait_send()
    pending.clear()

    @pl.when(i != j)
    def _():
        swap_copy.wait_send()

    def ladder_tile(n, _):
        rc, lc = n // 4, lax.rem(n, 4)
        rows = pl.ds(pl.multiple_of(rc * 512, 512), 512)
        cols = pl.ds(pl.multiple_of(lc * 512, 512), 512)
        x = jnp.dot(fac_l[rows, :], fac_r[:, cols], preferred_element_type=F32).astype(BF16)
        x = x.reshape(8, 2, 32, 512)
        even, odd = x[:, 0], x[:, 1]
        for v in range(8):
            lanes = slice(64 * v, 64 * v + 64)
            y = jnp.concatenate([even[:, :, lanes], odd[:, :, lanes]], axis=2)
            at = pl.multiple_of(lc * 256 + v * 32, 32)
            work[pl.ds(rc * 8, 8), pl.ds(at, 32), :] = y
        return 0

    lax.fori_loop(0, 16, ladder_tile, 0)
    get_amps.wait()

    axes = [(i, along_col, j, along_dev), (j, along_dev, i, along_col)]
    for q in range(4):
        pcols = slice(256 * q, 256 * q + 256)

        def sum_rows(n, _):
            rows = pl.ds(pl.multiple_of(n * 512, 512), 512)
            total = None
            for kc in range(4):
                x = jnp.concatenate([work[8 * kc + c, rows, :] for c in range(8)], axis=1)
                y = jnp.dot(x, amps[1024 * kc:1024 * kc + 1024, pcols], preferred_element_type=F32)
                total = y if total is None else total + y
            for half in range(2):
                sums[half, rows, :] = total[:, 128 * half:128 * half + 128]
            return 0

        lax.fori_loop(0, 2, sum_rows, 0)
        me, to, _, _ = axes[q % 2]
        for a in range(32):
            x = jnp.concatenate([sums[half, pl.ds(a, 32, stride=32), :] for half in range(2)], axis=1).astype(BF16)
            if q % 2 == 0:
                send1[q, a // 4, 32 * (a % 4):32 * (a % 4) + 32, :] = x
            else:
                for h in range(2):
                    send1[q, 2 * (a % 4) + h, 16 * (a // 4):16 * (a // 4) + 16, :] = x[16 * h:16 * h + 16]
        for d in range(1, 8):
            peer = lax.rem(me + d, 8)
            push(send1.at[q, peer], land1.at[q, me], rs_send.at[0, q, d], rs_recv.at[0, q, d], to(peer))

    for q in range(4):
        me, _, other, to = axes[q % 2]
        total = send1[q, me].astype(F32)
        for d in range(1, 8):
            src = lax.rem(me + 8 - d, 8)
            landed(land1.at[q, src], rs_recv.at[0, q, d])
            total = total + land1[q, src].astype(F32)
        send2[q] = total.astype(BF16).reshape(8, 16, 256)
        for d in range(1, 8):
            peer = lax.rem(other + d, 8)
            push(send2.at[q, peer], land2.at[q, other], rs_send.at[1, q, d], rs_recv.at[1, q, d], to(peer))

    for q in range(4):
        _, _, other, to = axes[q % 2]
        total = send2[q, other].astype(F32)
        for d in range(1, 8):
            src = lax.rem(other + 8 - d, 8)
            landed(land2.at[q, src], rs_recv.at[1, q, d])
            total = total + land2[q, src].astype(F32)
        out[:, 256 * q:256 * q + 256] = total

    for copy in pending:
        copy.wait_send()


def on_device(raw_ints, metric, amplitudes, pair_list, occ_energy, vir_energy, window_ids):
    width = raw_ints.shape[1]
    raw_ca = jnp.transpose(raw_ints, (2, 1, 0)).reshape(2048, 128)
    raw_bd = jnp.transpose(raw_ints, (1, 2, 0)).reshape(2048, 128)
    amp = amplitudes.reshape(4096, 1024)
    vmem = lambda shape, kind: pltpu.VMEM(shape, kind)
    dma = pltpu.SemaphoreType.DMA
    summed = pl.pallas_call(
        ladder_kernel,
        out_shape=jax.ShapeDtypeStruct((16, 1024), F32),
        in_specs=[pl.BlockSpec(memory_space=pl.ANY)] * 4,
        out_specs=pl.BlockSpec(memory_space=pltpu.VMEM),
        scratch_shapes=[
            vmem((32, 1024, 128), BF16),
            vmem((8, 128, 1024), BF16),
            vmem((2048, 1024), F32),
            vmem((1024, 2048), F32),
            vmem((2048, 1024), BF16),
            vmem((1024, 2048), BF16),
            vmem((4096, 1024), BF16),
            vmem((2, 1024, 128), F32),
            vmem((4, 8, 128, 256), BF16),
            vmem((4, 8, 128, 256), BF16),
            vmem((4, 8, 16, 256), BF16),
            vmem((4, 8, 16, 256), BF16),
            dma((6,)),
            dma((3, 10)), dma((3, 10)), dma((3, 10)), dma((3, 10)),
            dma((2, 4, 8)), dma((2, 4, 8)),
        ],
        compiler_params=pltpu.CompilerParams(
            collective_id=0, has_side_effects=True, vmem_limit_bytes=60 * 2**20
        ),
        cost_estimate=pl.CostEstimate(flops=26 * 10**9, bytes_accessed=10 * 10**6, transcendentals=0),
    )(raw_ca, raw_bd, metric, amp)
    row_total = summed.shape[0]
    global_rows = lax.axis_index(("col", "dev")) * row_total + jnp.arange(row_total, dtype=jnp.int32)
    window_energy = select_energy(window_ids, vir_energy)
    energy_first = select_energy(global_rows // width, window_energy)
    energy_second = select_energy(global_rows % width, window_energy)
    energy_i = select_energy(pair_list[0], occ_energy)
    energy_j = select_energy(pair_list[1], occ_energy)
    denominator = (energy_i + energy_j)[None, :] - (energy_first + energy_second)[:, None]
    return summed / denominator


def solution(mesh):
    in_specs = (
        P("dev", None, "col"),
        P("dev", None),
        P("col", "dev", "ao"),
        P(None, "ao"),
        P(),
        P(),
        P(),
    )
    out_specs = P(("col", "dev"), "ao")
    return jax.shard_map(
        on_device, mesh=mesh, in_specs=in_specs, out_specs=out_specs, check_vma=False
    )
```

time: 706 us -> 119 us (0.17)
  waiting for transfers between devices: 517 us -> 0 us
  Pallas kernels: 0 us -> 114 us
  local copies, waits for them, and re-layouts: 75.7 us -> 2.19 us
  blocking collectives: 63.3 us -> 0 us
  matrix products: 32.8 us -> 0 us
  between operations: 13.2 us -> 0.09 us
    reduce_scatter x1 -> x0, waiting for transfers between devices: 354 us -> none  [on_device(): lax.psum_scatter(partial_value, ('col', 'dev'), scatter_dimension=0, tile...]
    all_gather x3 -> x0, waiting for transfers between devices: 162 us -> none  [the longest x1 78.6 us: on_device(): raw_block = lax.all_gather(raw_ints, 'dev', axis=0, tiled=True)]
    pallas_call x0 -> x1, Pallas kernels: none -> 114 us  [on_device(): pl.pallas_call(ladder_kernel, out_shape=jax.ShapeDtypeStruct((16, 1024),...]
    reshape x3 -> x0, local copies, waits for them, and re-layouts: 64.5 us -> none  [the longest x2 41.9 us: on_device(): ladder = ladder_flat.reshape(full_width, c_block, full_width, d_block)]
    all_to_all x1 -> x0, blocking collectives: 63.3 us -> none  [on_device(): lax.all_to_all(spread, 'dev', split_axis=2, concat_axis=0, tiled=True)]
    dot_general x3 -> x0, matrix products: 32.8 us -> none  [the longest x1 15.1 us: on_device(): jnp.dot(ladder, amplitudes.reshape(c_block * d_block, amplitudes.shape[2]...]
  transfers between devices with their start and end apart: 4 -> 0, of which waited for: 4 -> 0; matrix products, arithmetic and copies ran while one was open for 1% -> 0% of each run, Pallas kernels for 0% -> 0%
where the time goes in v1:
time: 119 us; the launch traced here: 118 us
  Pallas kernels  114 us (96%)
  local copies, waits for them, and re-layouts  2.19 us (2%)
  other arithmetic  2.1 us (2%)
    pallas_call x1, Pallas kernels, on_device(): pl.pallas_call(ladder_kernel, out_shape=jax.ShapeDtypeStruct((16, 1024),...  114 us

profile of v1, /device:TPU:0, one launch (start us, length us, event | category | flops | bytes accessed | tf_op | source)
XLA Modules:
  0.0 118.0 jit_solution(2154575928007247707)
XLA Ops:
  0.0 2.2 %copy.9 = bf16[64,32,128]{2,1,0:T(8,128)(2,1)} copy(bf16[64,32,128]{2,0,1:T(8,128)(2,1)} %bitcast.8) | data formatting | bytes 1048576 | tf_op jit(solution)/shard_map/transpose | solution.py:323
  2.2 0.0 copy-start.1
  2.2 0.0 copy-start.3
  2.2 0.0 copy-start
  2.2 0.0 copy-start.2
  2.2 113.6 %shard_map.73 = f32[16,1024]{1,0:T(8,128)} custom-call(bf16[2048,128]{1,0:T(8,128)(2,1)} %bitcast.10, bf16[2048,128]{1,0:T(8,128)(2,1)} %bitcast.9, bf16[128,1024]{1,0:T(8,128)(2,1)} %met.1, bf16[4096,1024]{1,0:T(8,128)(2,1)} %bitcast.13), custom_call_target="tpu_custom_call" | custom-call | flops 25999998976 | bytes 10000000 | tf_op jit(solution)/shard_map/pallas_call | solution.py:328
  115.8 0.0 copy-done.1
  115.8 0.0 copy-done.3
  115.9 0.2 select_reduce_fusion.2
  116.0 0.2 select_reduce_fusion.3
  116.2 0.0 copy-done
  116.3 0.0 copy-done.2
  116.3 0.2 select_reduce_fusion
  116.4 1.6 %subtract_divide_fusion = f32[16,1024]{1,0:T(8,128)} fusion(f32[16,1024]{1,0:T(8,128)} %shard_map.73, f32[16]{0:T(128)S(1)} %add.50, f32[1024]{0:T(1024)S(1)} %add.45), kind=kLoop, calls=%fused_computation.4 | loop fusion | flops 32768 | bytes 135232 | tf_op jit(solution)/shard_map/div | solution.py:363
  (4 shorter events, 0.0 us)
Async XLA Ops:
  2.2 113.7 %copy-start.1 = (f32[512]{0:T(512)S(1)}, f32[512]{0:T(512)}, u32[]{:S(2)}) copy-start(f32[512]{0:T(512)} %param.12) | copy-start | bytes 6148
  2.2 113.7 %copy-start.3 = (s32[32]{0:T(128)S(1)}, s32[32]{0:T(128)}, u32[]{:S(2)}) copy-start(s32[32]{0:T(128)} %param.13) | copy-start | bytes 388
  2.2 114.1 %copy-start = (s32[2,1024]{1,0:T(2,128)S(1)}, s32[2,1024]{1,0:T(2,128)}, u32[]{:S(2)}) copy-start(s32[2,1024]{1,0:T(2,128)} %param.10) | copy-start | bytes 24580
  2.2 114.1 %copy-start.2 = (f32[64]{0:T(128)S(1)}, f32[64]{0:T(128)}, u32[]{:S(2)}) copy-start(f32[64]{0:T(128)} %param.11) | copy-start | bytes 772

commit v2 on v1

v2 whole, which is shorter than its diff:
```python
import jax
import jax.numpy as jnp
from jax import lax
from jax.experimental import pallas as pl
from jax.experimental.pallas import tpu as pltpu
from jax.sharding import PartitionSpec as P

MESH = pl.DeviceIdType.MESH
F32, BF16 = jnp.float32, jnp.bfloat16
NT = (((1,), (1,)), ((), ()))

PARTNER, MINUS, PLUS, MINUS_P, PLUS_P, FAR_A, FAR_AP, FAR_B, FAR_BP = range(9)
OWN = 9


def select_energy(positions, table):
    labels = jnp.arange(table.shape[0], dtype=jnp.int32)
    return jnp.sum(jnp.where(positions[:, None] == labels[None, :], table[None, :], 0.0), axis=1)


def ladder_kernel(
    raw_ca, raw_bd, met, amp, out,
    work, mbuf, acc_l, fac_l, fac_r, amps, sums, send1, land1, send2, land2,
    local_sem, deal_send, deal_recv, ag_send, ag_recv, rel_send, rel_recv, rs_send, rs_recv,
):
    i, j, o = lax.axis_index("col"), lax.axis_index("dev"), lax.axis_index("ao")
    flip = lambda g: lax.rem(g + 4, 8)
    ring = lambda g, step: (g // 4) * 4 + lax.rem(lax.rem(g, 4) + step, 4)
    along_dev = lambda g: (i, g, o)
    along_col = lambda g: (g, j, o)
    sibling = (i, j, 1 - o)
    u, v = lax.rem(i // 4 + j // 4, 2) * 4 + lax.rem(i, 4), j
    at = lambda u, v: (lax.rem(u // 4 + v // 4, 2) * 4 + lax.rem(u, 4), v, o)

    barrier = pltpu.get_barrier_semaphore()

    def greet(device):
        pl.semaphore_signal(barrier, inc=1, device_id=device, device_id_type=MESH)

    for d in (1, 3):
        greet(along_col(ring(i, d)))
        greet(along_dev(ring(j, d)))
    greet(along_col(flip(i)))
    greet(along_dev(flip(j)))
    greet((flip(i), flip(j), o))
    greet(sibling)
    diagonal = i == j
    for k in range(8):
        @pl.when(jnp.logical_not(diagonal & (j == k)))
        def _():
            greet((j, k, o))

    sums[...] = jnp.zeros_like(sums)
    pl.semaphore_wait(barrier, 16 - jnp.where(diagonal, 1, 0))

    pending = []

    def push(src, dst, send_sem, recv_sem, device):
        copy = pltpu.make_async_remote_copy(
            src_ref=src, dst_ref=dst, send_sem=send_sem, recv_sem=recv_sem,
            device_id=device, device_id_type=MESH,
        )
        copy.start()
        pending.append(copy)

    def landed(dst, recv_sem):
        pltpu.make_async_remote_copy(
            src_ref=dst, dst_ref=dst, send_sem=recv_sem, recv_sem=recv_sem,
            device_id=sibling, device_id_type=MESH,
        ).wait_recv()

    class Gather:
        def __init__(self, which, me, to, partner, half, part):
            self.which, self.me, self.half, self.part = which, me, half, part
            self.up, self.down = to(ring(me, 1)), to(ring(me, 3))
            self.partner = partner
            plus, minus, far = ring(me, 1), ring(me, 3), ring(me, 2)
            self.plus, self.minus, self.far = plus, minus, far
            self.place = {
                PARTNER: (flip(me), None), MINUS: (minus, None), PLUS: (plus, None),
                MINUS_P: (flip(minus), None), PLUS_P: (flip(plus), None),
                FAR_A: (far, 0), FAR_AP: (flip(far), 0), FAR_B: (far, 1), FAR_BP: (flip(far), 1),
            }

        def spot(self, kind, core):
            piece, quarter = self.place[kind]
            if quarter is None:
                return self.half(piece, core)
            return self.part(piece, core, quarter)

        def send(self, src, dst, kind, device):
            push(src, dst, ag_send.at[self.which, kind], ag_recv.at[self.which, kind], device)

        def send_own(self, src):
            dst = self.half(self.me, o)
            self.send(src, dst, MINUS, self.up)
            self.send(src, dst, PLUS, self.down)
            self.send(src, dst, PARTNER, self.partner)

        def arrive(self, *kinds):
            for kind in kinds:
                spot = self.spot(kind, o)
                landed(spot, ag_recv.at[self.which, kind])
                piece = self.place[kind][0]
                if self.which == 2 and kind in (MINUS, PLUS, FAR_A, FAR_B):
                    self.send(spot, spot, {MINUS: MINUS_P, PLUS: PLUS_P, FAR_A: FAR_AP, FAR_B: FAR_BP}[kind], self.partner)
                if self.which != 2 and kind == PARTNER:
                    self.send(spot, spot, MINUS_P, self.up)
                    self.send(spot, spot, PLUS_P, self.down)
                elif kind == MINUS or self.which != 2 and kind == MINUS_P:
                    first = self.part(piece, o, 0)
                    self.send(first, first, FAR_A if kind == MINUS else FAR_AP, self.up)
                elif kind == PLUS or self.which != 2 and kind == PLUS_P:
                    second = self.part(piece, o, 1)
                    self.send(second, second, FAR_B if kind == PLUS else FAR_BP, self.down)
                push(spot, spot, rel_send.at[self.which, kind], rel_recv.at[self.which, kind], sibling)

        def from_sibling(self, *kinds):
            for kind in kinds:
                landed(self.spot(kind, 1 - o), rel_recv.at[self.which, kind])

    left = Gather(
        0, j, along_dev, along_dev(flip(j)),
        lambda k, core: work.at[2 * k + core],
        lambda k, core, q: work.at[2 * k + core, pl.ds(512 * q, 512)],
    )
    right = Gather(
        1, i, along_col, along_col(flip(i)),
        lambda k, core: work.at[16 + 2 * k + core],
        lambda k, core, q: work.at[16 + 2 * k + core, pl.ds(512 * q, 512)],
    )
    fit = Gather(
        2, j, along_dev, (flip(i), flip(j), o),
        lambda k, core: mbuf.at[k, pl.ds(pl.multiple_of(64 * core, 64), 64)],
        lambda k, core, q: mbuf.at[k, pl.ds(pl.multiple_of(64 * core + 32 * q, 32), 32)],
    )

    own_half = pl.ds(pl.multiple_of(1024 * o, 1024), 1024)
    fit.send_own(met.at[pl.ds(pl.multiple_of(64 * o, 64), 64)])
    chunk = lambda g: raw_bd.at[pl.ds(pl.multiple_of(256 * g + 128 * o, 128), 128)]
    chunk_at = lambda g, k: work.at[16 + 2 * g + o, pl.ds(pl.multiple_of(128 * k, 128), 128)]
    for d in range(8):
        g = lax.rem(i + d, 8)

        @pl.when(jnp.logical_not(diagonal & (g == i)))
        def _():
            pltpu.make_async_remote_copy(
                src_ref=chunk(g), dst_ref=chunk_at(g, j), send_sem=deal_send.at[g],
                recv_sem=deal_recv.at[j], device_id=(g, i, o), device_id_type=MESH,
            ).start()

    @pl.when(diagonal)
    def _():
        here = pltpu.make_async_copy(chunk(i), chunk_at(i, j), local_sem.at[3])
        here.start()
        here.wait()

    left.send_own(raw_ca.at[own_half])

    own_l = [
        pltpu.make_async_copy(raw_ca.at[pl.ds(1024 * h, 1024)], work.at[2 * j + h], local_sem.at[4 + h])
        for h in range(2)
    ]
    own_m = pltpu.make_async_copy(met, mbuf.at[j], local_sem.at[1])
    get_amps = pltpu.make_async_copy(amp, amps, local_sem.at[2])
    for copy in own_l + [own_m, get_amps]:
        copy.start()

    fit.arrive(PARTNER)
    left.arrive(PARTNER)

    for k in range(8):
        @pl.when(jnp.logical_not(diagonal & (j == k)))
        def _():
            landed(chunk_at(i, k), deal_recv.at[k])

    own_chunk = work.at[16 + 2 * i + o]
    right.send_own(own_chunk)
    push(own_chunk, own_chunk, rel_send.at[1, OWN], rel_recv.at[1, OWN], sibling)
    fit.arrive(MINUS, PLUS)
    left.arrive(MINUS, PLUS)
    fit.arrive(FAR_A, FAR_B)
    right.arrive(PARTNER)
    fit.arrive(MINUS_P, PLUS_P)
    left.arrive(MINUS_P, PLUS_P)
    right.arrive(MINUS, PLUS)
    fit.arrive(FAR_AP, FAR_BP)
    for copy in own_l + [own_m]:
        copy.wait()
    fit.from_sibling(*range(9))

    def m_slice(k):
        return mbuf[:, :, pl.ds(pl.multiple_of(k * 128, 128), 128)].reshape(1024, 128)

    def fit_left(pieces, first=False, last=False):
        m = jnp.concatenate([m_slice(k) for k in pieces], axis=1)

        def body(n, _):
            rows = pl.ds(pl.multiple_of(n * 1024, 1024), 1024)
            x = jnp.concatenate([work[2 * k + n] for k in pieces], axis=1)
            y = lax.dot_general(x, m, NT, preferred_element_type=F32)
            if not first:
                y = y + acc_l[rows, :]
            if last:
                fac_l[rows, :] = y.astype(BF16)
            else:
                acc_l[rows, :] = y
            return 0

        lax.fori_loop(0, 2, body, 0)

    def fit_right(count, piece_of):
        def body(n, _):
            one = piece_of(n)
            two = flip(one)
            x = jnp.concatenate([
                jnp.concatenate([work[16 + 2 * g + h, 128 * k:128 * k + 128, :] for k in range(8)], axis=1)
                for g in (one, two) for h in range(2)
            ], axis=0)
            y = lax.dot_general(mbuf[...].reshape(1024, 1024), x, NT, preferred_element_type=F32).astype(BF16)
            fac_r[:, pl.ds(pl.multiple_of(256 * one, 256), 256)] = y[:, :256]
            fac_r[:, pl.ds(pl.multiple_of(256 * two, 256), 256)] = y[:, 256:]
            return 0

        lax.fori_loop(0, count, body, 0)

    left.from_sibling(PARTNER)
    fit_left([left.me, flip(left.me)], first=True)
    right.arrive(MINUS_P, PLUS_P)
    landed(work.at[16 + 2 * i + 1 - o], rel_recv.at[1, OWN])
    right.from_sibling(PARTNER)
    fit_right(1, lambda n: i)
    left.from_sibling(MINUS, MINUS_P, PLUS, PLUS_P)
    fit_left([left.minus, flip(left.minus), left.plus, flip(left.plus)])
    left.arrive(FAR_A, FAR_B, FAR_AP, FAR_BP)
    right.from_sibling(MINUS, MINUS_P, PLUS, PLUS_P)
    fit_right(2, lambda n: ring(i, 1 + 2 * n))
    right.arrive(FAR_A, FAR_B, FAR_AP, FAR_BP)
    left.from_sibling(FAR_A, FAR_B, FAR_AP, FAR_BP)
    fit_left([left.far, flip(left.far)], last=True)
    right.from_sibling(FAR_A, FAR_B, FAR_AP, FAR_BP)
    fit_right(1, lambda n: right.far)

    for copy in pending:
        copy.wait_send()
    pending.clear()

    for g in range(8):
        @pl.when(jnp.logical_not(diagonal & (g == i)))
        def _():
            pltpu.make_async_remote_copy(
                src_ref=chunk(g), dst_ref=chunk_at(g, j), send_sem=deal_send.at[g],
                recv_sem=deal_recv.at[j], device_id=(g, i, o), device_id_type=MESH,
            ).wait_send()

    def ladder_tile(n, _):
        rc, lc = n // 2, lax.rem(n, 2)
        rows = pl.ds(pl.multiple_of(rc * 512, 512), 512)
        cols = pl.ds(pl.multiple_of(lc * 1024, 1024), 1024)
        x = jnp.dot(fac_l[rows, :], fac_r[:, cols], preferred_element_type=F32).astype(BF16)
        x = x.reshape(8, 2, 32, 1024)
        even, odd = x[:, 0], x[:, 1]
        for v in range(16):
            lanes = slice(64 * v, 64 * v + 64)
            y = jnp.concatenate([even[:, :, lanes], odd[:, :, lanes]], axis=2)
            at = pl.multiple_of(lc * 512 + v * 32, 32)
            work[pl.ds(rc * 8, 8), pl.ds(at, 32), :] = y
        return 0

    lax.fori_loop(0, 8, ladder_tile, 0)
    get_amps.wait()

    def route(stage, c):
        if (c + stage) % 2 == 0:
            return u, lambda g: at(g, v)
        return v, lambda g: at(u, g)

    def spread(stage, c, src, dst):
        me, to = route(stage, c)
        for d in (1, 7, 4, 3, 5, 2, 6):
            peer = lax.rem(me + d, 8)
            push(src.at[c, peer], dst.at[c, d - 1], rs_send.at[stage, c, d - 1], rs_recv.at[stage, c, d - 1], to(peer))

    def collect(stage, c, src, dst):
        total = src[c, route(stage, c)[0]].astype(F32)
        for d in range(7):
            landed(dst.at[c, d], rs_recv.at[stage, c, d])
            total = total + dst[c, d].astype(F32)
        return total

    def quarter(q):
        def deep(kc, _):
            lhs = jnp.concatenate([work[16 * kc + c] for c in range(16)], axis=1)
            rhs = amps[pl.ds(pl.multiple_of(2048 * kc, 2048), 2048), 256 * q:256 * q + 256]
            y = jnp.dot(lhs, rhs, preferred_element_type=F32)
            for half in range(2):
                part = y[:, 128 * half:128 * half + 128]
                sums[half] = part + jnp.where(kc == 0, 0.0, sums[half])
            return 0

        lax.fori_loop(0, 2, deep, 0)
        for half in range(2):
            c = 2 * q + half
            for a in range(32):
                value = sums[half, pl.ds(a, 32, stride=32), :].astype(BF16)
                for h in range(2):
                    k = 2 * a + h
                    ku, kv = (k // 32 + k // 4) % 2 * 4 + k // 8 % 4, k % 8
                    one, two = (ku, kv) if c % 2 == 0 else (kv, ku)
                    send1[c, one, 16 * two:16 * two + 16, :] = value[16 * h:16 * h + 16]
            spread(0, c, send1, land1)

    def second(c):
        send2[c] = collect(0, c, send1, land1).astype(BF16).reshape(8, 16, 128)
        spread(1, c, send2, land2)

    quarter(0)
    quarter(1)
    quarter(2)
    second(0)
    second(1)
    quarter(3)
    for c in range(2, 8):
        second(c)
    for c in range(8):
        out[:, 128 * c:128 * c + 128] = collect(1, c, send2, land2)

    for copy in pending:
        copy.wait_send()


def on_device(raw_ints, metric, amplitudes, pair_list, occ_energy, vir_energy, window_ids):
    width = raw_ints.shape[1]
    raw_ca = jnp.transpose(raw_ints, (2, 1, 0)).reshape(2048, 128)
    raw_bd = jnp.transpose(raw_ints, (1, 2, 0)).reshape(2048, 128)
    amp = amplitudes.reshape(4096, 1024)
    vmem = lambda shape, kind: pltpu.VMEM(shape, kind)
    dma = pltpu.SemaphoreType.DMA
    summed = pl.pallas_call(
        ladder_kernel,
        out_shape=jax.ShapeDtypeStruct((16, 1024), F32),
        in_specs=[pl.BlockSpec(memory_space=pl.ANY)] * 4,
        out_specs=pl.BlockSpec(memory_space=pltpu.VMEM),
        scratch_shapes=[
            vmem((32, 1024, 128), BF16),
            vmem((8, 128, 1024), BF16),
            vmem((2048, 1024), F32),
            vmem((2048, 1024), BF16),
            vmem((1024, 2048), BF16),
            vmem((4096, 1024), BF16),
            vmem((2, 1024, 128), F32),
            vmem((8, 8, 128, 128), BF16),
            vmem((8, 7, 128, 128), BF16),
            vmem((8, 8, 16, 128), BF16),
            vmem((8, 7, 16, 128), BF16),
            dma((6,)), dma((8,)), dma((8,)),
            dma((3, 9)), dma((3, 9)), dma((3, 10)), dma((3, 10)),
            dma((2, 8, 7)), dma((2, 8, 7)),
        ],
        compiler_params=pltpu.CompilerParams(
            collective_id=0, has_side_effects=True, vmem_limit_bytes=60 * 2**20
        ),
        cost_estimate=pl.CostEstimate(flops=26 * 10**9, bytes_accessed=10 * 10**6, transcendentals=0),
    )(raw_ca, raw_bd, metric, amp)
    row_total = summed.shape[0]
    global_rows = lax.axis_index(("col", "dev")) * row_total + jnp.arange(row_total, dtype=jnp.int32)
    window_energy = select_energy(window_ids, vir_energy)
    energy_first = select_energy(global_rows // width, window_energy)
    energy_second = select_energy(global_rows % width, window_energy)
    energy_i = select_energy(pair_list[0], occ_energy)
    energy_j = select_energy(pair_list[1], occ_energy)
    denominator = (energy_i + energy_j)[None, :] - (energy_first + energy_second)[:, None]
    return summed / denominator


def solution(mesh):
    in_specs = (
        P("dev", None, "col"),
        P("dev", None),
        P("col", "dev", "ao"),
        P(None, "ao"),
        P(),
        P(),
        P(),
    )
    out_specs = P(("col", "dev"), "ao")
    return jax.shard_map(
        on_device, mesh=mesh, in_specs=in_specs, out_specs=out_specs, check_vma=False
    )
```

time: 119 us -> 92.2 us (0.77)
  Pallas kernels: 114 us -> 87.5 us
    pallas_call x1, Pallas kernels: 114 us -> 87.5 us  [on_device(): pl.pallas_call(ladder_kernel, out_shape=jax.ShapeDtypeStruct((16, 1024),...]
where the time goes in v2:
time: 92.2 us; the launch traced here: 91.9 us
  Pallas kernels  87.5 us (95%)
  local copies, waits for them, and re-layouts  2.19 us (2%)
  other arithmetic  2.1 us (2%)
    pallas_call x1, Pallas kernels, on_device(): pl.pallas_call(ladder_kernel, out_shape=jax.ShapeDtypeStruct((16, 1024),...  87.5 us
    transpose x1, local copies, waits for them, and re-layouts, on_device(): raw_ca = jnp.transpose(raw_ints, (2, 1, 0)).reshape(2048, 128)  2.17 us

profile of v2, /device:TPU:0, one launch (start us, length us, event | category | flops | bytes accessed | tf_op | source)
XLA Modules:
  0.0 91.9 jit_solution(2107913084790853803)
XLA Ops:
  0.0 2.2 %copy.9 = bf16[64,32,128]{2,1,0:T(8,128)(2,1)} copy(bf16[64,32,128]{2,0,1:T(8,128)(2,1)} %bitcast.8) | data formatting | bytes 1048576 | tf_op jit(solution)/shard_map/transpose | solution.py:334
  2.2 0.0 copy-start.1
  2.2 0.0 copy-start.3
  2.2 0.0 copy-start
  2.2 0.0 copy-start.2
  2.2 87.5 %shard_map.73 = f32[16,1024]{1,0:T(8,128)} custom-call(bf16[2048,128]{1,0:T(8,128)(2,1)} %bitcast.10, bf16[2048,128]{1,0:T(8,128)(2,1)} %bitcast.9, bf16[128,1024]{1,0:T(8,128)(2,1)} %met.1, bf16[4096,1024]{1,0:T(8,128)(2,1)} %bitcast.13), custom_call_target="tpu_custom_call" | custom-call | flops 25999998976 | bytes 10000000 | tf_op jit(solution)/shard_map/pallas_call | solution.py:339
  89.8 0.0 copy-done.1
  89.8 0.0 copy-done.3
  89.8 0.2 select_reduce_fusion.2
  90.0 0.2 select_reduce_fusion.3
  90.2 0.0 copy-done
  90.2 0.0 copy-done.2
  90.2 0.2 select_reduce_fusion
  90.4 1.6 %subtract_divide_fusion = f32[16,1024]{1,0:T(8,128)} fusion(f32[16,1024]{1,0:T(8,128)} %shard_map.73, f32[16]{0:T(128)S(1)} %add.50, f32[1024]{0:T(1024)S(1)} %add.45), kind=kLoop, calls=%fused_computation.4 | loop fusion | flops 32768 | bytes 135232 | tf_op jit(solution)/shard_map/div | solution.py:373
  (4 shorter events, 0.0 us)
Async XLA Ops:
  2.2 87.6 %copy-start.1 = (f32[512]{0:T(512)S(1)}, f32[512]{0:T(512)}, u32[]{:S(2)}) copy-start(f32[512]{0:T(512)} %param.12) | copy-start | bytes 6148
  2.2 87.6 %copy-start.3 = (s32[32]{0:T(128)S(1)}, s32[32]{0:T(128)}, u32[]{:S(2)}) copy-start(s32[32]{0:T(128)} %param.13) | copy-start | bytes 388
  2.2 88.0 %copy-start = (s32[2,1024]{1,0:T(2,128)S(1)}, s32[2,1024]{1,0:T(2,128)}, u32[]{:S(2)}) copy-start(s32[2,1024]{1,0:T(2,128)} %param.10) | copy-start | bytes 24580
  2.2 88.0 %copy-start.2 = (f32[64]{0:T(128)S(1)}, f32[64]{0:T(128)}, u32[]{:S(2)}) copy-start(f32[64]{0:T(128)} %param.11) | copy-start | bytes 772

commit v3 on v2

--- a/solution.py
+++ b/solution.py
@@ -19,8 +19,8 @@
 
 
 def ladder_kernel(
-    raw_ca, raw_bd, met, amp, out,
-    work, mbuf, acc_l, fac_l, fac_r, amps, sums, send1, land1, send2, land2,
+    raw_bd, met, amp, out,
+    raw, ladder, work, mbuf, acc_l, fac_l, fac_r, amps, sums, send1, land1, send2, land2,
     local_sem, deal_send, deal_recv, ag_send, ag_recv, rel_send, rel_recv, rs_send, rs_recv,
 ):
     i, j, o = lax.axis_index("col"), lax.axis_index("dev"), lax.axis_index("ao")
@@ -31,6 +31,13 @@
     sibling = (i, j, 1 - o)
     u, v = lax.rem(i // 4 + j // 4, 2) * 4 + lax.rem(i, 4), j
     at = lambda u, v: (lax.rem(u // 4 + v // 4, 2) * 4 + lax.rem(u, 4), v, o)
+
+    get_raw = pltpu.make_async_copy(raw_bd, raw, local_sem.at[0])
+    get_raw.start()
+    own_m = pltpu.make_async_copy(met, mbuf.at[j], local_sem.at[1])
+    own_m.start()
+    get_amps = pltpu.make_async_copy(amp, amps, local_sem.at[2])
+    get_amps.start()
 
     barrier = pltpu.get_barrier_semaphore()
 
@@ -50,7 +57,15 @@
         def _():
             greet((j, k, o))
 
+    get_raw.wait()
     sums[...] = jnp.zeros_like(sums)
+    for half in range(2):
+        for a in range(16):
+            row = 1024 * half + 64 * a
+            sums[half, 72 * a:72 * a + 64, :] = raw[row:row + 64, :].astype(F32)
+    for c in range(64):
+        rows = jnp.concatenate([sums[half, pl.ds(c, 16, stride=72), :] for half in range(2)], axis=0)
+        work[2 * j + c // 32, 32 * (c % 32):32 * (c % 32) + 32, :] = rows.astype(BF16)
     pl.semaphore_wait(barrier, 16 - jnp.where(diagonal, 1, 0))
 
     pending = []
@@ -102,15 +117,13 @@
                 spot = self.spot(kind, o)
                 landed(spot, ag_recv.at[self.which, kind])
                 piece = self.place[kind][0]
-                if self.which == 2 and kind in (MINUS, PLUS, FAR_A, FAR_B):
-                    self.send(spot, spot, {MINUS: MINUS_P, PLUS: PLUS_P, FAR_A: FAR_AP, FAR_B: FAR_BP}[kind], self.partner)
-                if self.which != 2 and kind == PARTNER:
+                if kind == PARTNER:
                     self.send(spot, spot, MINUS_P, self.up)
                     self.send(spot, spot, PLUS_P, self.down)
-                elif kind == MINUS or self.which != 2 and kind == MINUS_P:
+                elif kind in (MINUS, MINUS_P):
                     first = self.part(piece, o, 0)
                     self.send(first, first, FAR_A if kind == MINUS else FAR_AP, self.up)
-                elif kind == PLUS or self.which != 2 and kind == PLUS_P:
+                elif kind in (PLUS, PLUS_P):
                     second = self.part(piece, o, 1)
                     self.send(second, second, FAR_B if kind == PLUS else FAR_BP, self.down)
                 push(spot, spot, rel_send.at[self.which, kind], rel_recv.at[self.which, kind], sibling)
@@ -135,9 +148,8 @@
         lambda k, core, q: mbuf.at[k, pl.ds(pl.multiple_of(64 * core + 32 * q, 32), 32)],
     )
 
-    own_half = pl.ds(pl.multiple_of(1024 * o, 1024), 1024)
     fit.send_own(met.at[pl.ds(pl.multiple_of(64 * o, 64), 64)])
-    chunk = lambda g: raw_bd.at[pl.ds(pl.multiple_of(256 * g + 128 * o, 128), 128)]
+    chunk = lambda g: raw.at[pl.ds(pl.multiple_of(256 * g + 128 * o, 128), 128)]
     chunk_at = lambda g, k: work.at[16 + 2 * g + o, pl.ds(pl.multiple_of(128 * k, 128), 128)]
     for d in range(8):
         g = lax.rem(i + d, 8)
@@ -155,20 +167,8 @@
         here.start()
         here.wait()
 
-    left.send_own(raw_ca.at[own_half])
-
-    own_l = [
-        pltpu.make_async_copy(raw_ca.at[pl.ds(1024 * h, 1024)], work.at[2 * j + h], local_sem.at[4 + h])
-        for h in range(2)
-    ]
-    own_m = pltpu.make_async_copy(met, mbuf.at[j], local_sem.at[1])
-    get_amps = pltpu.make_async_copy(amp, amps, local_sem.at[2])
-    for copy in own_l + [own_m, get_amps]:
-        copy.start()
-
-    fit.arrive(PARTNER)
-    left.arrive(PARTNER)
-
+    fit.arrive(PARTNER, MINUS, PLUS)
+    left.send_own(work.at[2 * j + o])
     for k in range(8):
         @pl.when(jnp.logical_not(diagonal & (j == k)))
         def _():
@@ -177,16 +177,13 @@
     own_chunk = work.at[16 + 2 * i + o]
     right.send_own(own_chunk)
     push(own_chunk, own_chunk, rel_send.at[1, OWN], rel_recv.at[1, OWN], sibling)
-    fit.arrive(MINUS, PLUS)
-    left.arrive(MINUS, PLUS)
-    fit.arrive(FAR_A, FAR_B)
+    fit.arrive(MINUS_P, PLUS_P)
+    left.arrive(PARTNER)
     right.arrive(PARTNER)
-    fit.arrive(MINUS_P, PLUS_P)
-    left.arrive(MINUS_P, PLUS_P)
+    fit.arrive(FAR_A, FAR_B, FAR_AP, FAR_BP)
+    left.arrive(MINUS, PLUS, MINUS_P, PLUS_P)
     right.arrive(MINUS, PLUS)
-    fit.arrive(FAR_AP, FAR_BP)
-    for copy in own_l + [own_m]:
-        copy.wait()
+    own_m.wait()
     fit.from_sibling(*range(9))
 
     def m_slice(k):
@@ -224,6 +221,22 @@
 
         lax.fori_loop(0, count, body, 0)
 
+    def ladder_columns(pairs, piece_of):
+        def body(n, _):
+            g = piece_of(n // 2)
+            g = lax.rem(g + 4 * lax.rem(n, 2), 8)
+            cols = pl.ds(pl.multiple_of(256 * g, 256), 256)
+            x = jnp.dot(fac_l[...], fac_r[:, cols], preferred_element_type=F32).astype(BF16)
+            x = x.reshape(32, 2, 32, 256)
+            even, odd = x[:, 0], x[:, 1]
+            for n in range(4):
+                lanes = slice(64 * n, 64 * n + 64)
+                y = jnp.concatenate([even[:, :, lanes], odd[:, :, lanes]], axis=2)
+                ladder[:, pl.ds(pl.multiple_of(128 * g + 32 * n, 32), 32), :] = y
+            return 0
+
+        lax.fori_loop(0, 2 * pairs, body, 0)
+
     left.from_sibling(PARTNER)
     fit_left([left.me, flip(left.me)], first=True)
     right.arrive(MINUS_P, PLUS_P)
@@ -235,39 +248,14 @@
     left.arrive(FAR_A, FAR_B, FAR_AP, FAR_BP)
     right.from_sibling(MINUS, MINUS_P, PLUS, PLUS_P)
     fit_right(2, lambda n: ring(i, 1 + 2 * n))
-    right.arrive(FAR_A, FAR_B, FAR_AP, FAR_BP)
     left.from_sibling(FAR_A, FAR_B, FAR_AP, FAR_BP)
     fit_left([left.far, flip(left.far)], last=True)
+    ladder_columns(1, lambda n: i)
+    right.arrive(FAR_A, FAR_B, FAR_AP, FAR_BP)
+    ladder_columns(2, lambda n: ring(i, 1 + 2 * n))
     right.from_sibling(FAR_A, FAR_B, FAR_AP, FAR_BP)
     fit_right(1, lambda n: right.far)
-
-    for copy in pending:
-        copy.wait_send()
-    pending.clear()
-
-    for g in range(8):
-        @pl.when(jnp.logical_not(diagonal & (g == i)))
-        def _():
-            pltpu.make_async_remote_copy(
-                src_ref=chunk(g), dst_ref=chunk_at(g, j), send_sem=deal_send.at[g],
-                recv_sem=deal_recv.at[j], device_id=(g, i, o), device_id_type=MESH,
-            ).wait_send()
-
-    def ladder_tile(n, _):
-        rc, lc = n // 2, lax.rem(n, 2)
-        rows = pl.ds(pl.multiple_of(rc * 512, 512), 512)
-        cols = pl.ds(pl.multiple_of(lc * 1024, 1024), 1024)
-        x = jnp.dot(fac_l[rows, :], fac_r[:, cols], preferred_element_type=F32).astype(BF16)
-        x = x.reshape(8, 2, 32, 1024)
-        even, odd = x[:, 0], x[:, 1]
-        for v in range(16):
-            lanes = slice(64 * v, 64 * v + 64)
-            y = jnp.concatenate([even[:, :, lanes], odd[:, :, lanes]], axis=2)
-            at = pl.multiple_of(lc * 512 + v * 32, 32)
-            work[pl.ds(rc * 8, 8), pl.ds(at, 32), :] = y
-        return 0
-
-    lax.fori_loop(0, 8, ladder_tile, 0)
+    ladder_columns(1, lambda n: right.far)
     get_amps.wait()
 
     def route(stage, c):
@@ -290,19 +278,21 @@
 
     def quarter(q):
         def deep(kc, _):
-            lhs = jnp.concatenate([work[16 * kc + c] for c in range(16)], axis=1)
+            lhs = jnp.concatenate([ladder[16 * kc + c] for c in range(16)], axis=1)
             rhs = amps[pl.ds(pl.multiple_of(2048 * kc, 2048), 2048), 256 * q:256 * q + 256]
             y = jnp.dot(lhs, rhs, preferred_element_type=F32)
             for half in range(2):
                 part = y[:, 128 * half:128 * half + 128]
-                sums[half] = part + jnp.where(kc == 0, 0.0, sums[half])
+                for b in range(32):
+                    at_b = slice(40 * b, 40 * b + 32)
+                    sums[half, at_b, :] = part[32 * b:32 * b + 32] + jnp.where(kc == 0, 0.0, sums[half, at_b, :])
             return 0
 
         lax.fori_loop(0, 2, deep, 0)
         for half in range(2):
             c = 2 * q + half
             for a in range(32):
-                value = sums[half, pl.ds(a, 32, stride=32), :].astype(BF16)
+                value = sums[half, pl.ds(a, 32, stride=40), :].astype(BF16)
                 for h in range(2):
                     k = 2 * a + h
                     ku, kv = (k // 32 + k // 4) % 2 * 4 + k // 8 % 4, k % 8
@@ -327,11 +317,17 @@
 
     for copy in pending:
         copy.wait_send()
+    for g in range(8):
+        @pl.when(jnp.logical_not(diagonal & (g == i)))
+        def _():
+            pltpu.make_async_remote_copy(
+                src_ref=chunk(g), dst_ref=chunk_at(g, j), send_sem=deal_send.at[g],
+                recv_sem=deal_recv.at[j], device_id=(g, i, o), device_id_type=MESH,
+            ).wait_send()
 
 
 def on_device(raw_ints, metric, amplitudes, pair_list, occ_energy, vir_energy, window_ids):
     width = raw_ints.shape[1]
-    raw_ca = jnp.transpose(raw_ints, (2, 1, 0)).reshape(2048, 128)
     raw_bd = jnp.transpose(raw_ints, (1, 2, 0)).reshape(2048, 128)
     amp = amplitudes.reshape(4096, 1024)
     vmem = lambda shape, kind: pltpu.VMEM(shape, kind)
@@ -339,16 +335,18 @@
     summed = pl.pallas_call(
         ladder_kernel,
         out_shape=jax.ShapeDtypeStruct((16, 1024), F32),
-        in_specs=[pl.BlockSpec(memory_space=pl.ANY)] * 4,
+        in_specs=[pl.BlockSpec(memory_space=pl.ANY)] * 3,
         out_specs=pl.BlockSpec(memory_space=pltpu.VMEM),
         scratch_shapes=[
+            vmem((2048, 128), BF16),
+            vmem((32, 1024, 128), BF16),
             vmem((32, 1024, 128), BF16),
             vmem((8, 128, 1024), BF16),
             vmem((2048, 1024), F32),
             vmem((2048, 1024), BF16),
             vmem((1024, 2048), BF16),
             vmem((4096, 1024), BF16),
-            vmem((2, 1024, 128), F32),
+            vmem((2, 1280, 128), F32),
             vmem((8, 8, 128, 128), BF16),
             vmem((8, 7, 128, 128), BF16),
             vmem((8, 8, 16, 128), BF16),
@@ -361,7 +359,7 @@
             collective_id=0, has_side_effects=True, vmem_limit_bytes=60 * 2**20
         ),
         cost_estimate=pl.CostEstimate(flops=26 * 10**9, bytes_accessed=10 * 10**6, transcendentals=0),
-    )(raw_ca, raw_bd, metric, amp)
+    )(raw_bd, metric, amp)
     row_total = summed.shape[0]
     global_rows = lax.axis_index(("col", "dev")) * row_total + jnp.arange(row_total, dtype=jnp.int32)
     window_energy = select_energy(window_ids, vir_energy)

time: 92.2 us -> 88.4 us (0.959)
  Pallas kernels: 87.5 us -> 83.9 us
  local copies, waits for them, and re-layouts: 2.19 us -> 0.78 us
  other arithmetic: 2.1 us -> 3.44 us
    pallas_call x1, Pallas kernels: 87.5 us -> 83.9 us  [on_device(): pl.pallas_call(ladder_kernel, out_shape=jax.ShapeDtypeStruct((16, 1024),...]
    transpose x1 -> x0, local copies, waits for them, and re-layouts: 2.17 us -> none  [on_device(): raw_ca = jnp.transpose(raw_ints, (2, 1, 0)).reshape(2048, 128)]
    reduce_sum x3, other arithmetic: 0.52 us -> 1.86 us  [select_energy(): jnp.sum(jnp.where(positions[:, None] == labels[None, :], table[None, :],...]
where the time goes in v3:
time: 88.4 us; the launch traced here: 88.2 us
  Pallas kernels  83.9 us (95%)
  other arithmetic  3.44 us (4%)
    pallas_call x1, Pallas kernels, on_device(): pl.pallas_call(ladder_kernel, out_shape=jax.ShapeDtypeStruct((16, 1024),...  83.9 us
    reduce_sum x3, other arithmetic, select_energy(): jnp.sum(jnp.where(positions[:, None] == labels[None, :], table[None, :],...  1.86 us

profile of v3, /device:TPU:0, one launch (start us, length us, event | category | flops | bytes accessed | tf_op | source)
XLA Modules:
  0.0 88.2 jit_solution(5546998201091883919)
XLA Ops:
  0.0 0.9 select_reduce_fusion.2
  0.9 0.2 select_reduce_fusion.3
  1.1 0.8 fusion
  1.9 0.8 select_reduce_fusion
  2.7 83.9 %shard_map.73 = f32[16,1024]{1,0:T(8,128)} custom-call(bf16[2048,128]{1,0:T(8,128)(2,1)} %bitcast.9, bf16[128,1024]{1,0:T(8,128)(2,1)} %met.1, bf16[4096,1024]{1,0:T(8,128)(2,1)} %bitcast.8), custom_call_target="tpu_custom_call" | custom-call | flops 25999998976 | bytes 10000000 | tf_op jit(solution)/shard_map/pallas_call | solution.py:335
  86.6 1.6 %subtract_divide_fusion = f32[16,1024]{1,0:T(8,128)} fusion(f32[16,1024]{1,0:T(8,128)} %shard_map.73, f32[16]{0:T(128)S(1)} %add.50, f32[1024]{0:T(1024)S(1)} %add.45), kind=kLoop, calls=%fused_computation.4 | loop fusion | flops 32768 | bytes 135232 | tf_op jit(solution)/shard_map/div | solution.py:371
  (3 shorter events, 0.0 us)

commit v4 on v3

--- a/solution.py
+++ b/solution.py
@@ -148,7 +148,6 @@
         lambda k, core, q: mbuf.at[k, pl.ds(pl.multiple_of(64 * core + 32 * q, 32), 32)],
     )
 
-    fit.send_own(met.at[pl.ds(pl.multiple_of(64 * o, 64), 64)])
     chunk = lambda g: raw.at[pl.ds(pl.multiple_of(256 * g + 128 * o, 128), 128)]
     chunk_at = lambda g, k: work.at[16 + 2 * g + o, pl.ds(pl.multiple_of(128 * k, 128), 128)]
     for d in range(8):
@@ -160,6 +159,8 @@
                 src_ref=chunk(g), dst_ref=chunk_at(g, j), send_sem=deal_send.at[g],
                 recv_sem=deal_recv.at[j], device_id=(g, i, o), device_id_type=MESH,
             ).start()
+
+    fit.send_own(met.at[pl.ds(pl.multiple_of(64 * o, 64), 64)])
 
     @pl.when(diagonal)
     def _():
@@ -229,10 +230,14 @@
             x = jnp.dot(fac_l[...], fac_r[:, cols], preferred_element_type=F32).astype(BF16)
             x = x.reshape(32, 2, 32, 256)
             even, odd = x[:, 0], x[:, 1]
-            for n in range(4):
-                lanes = slice(64 * n, 64 * n + 64)
-                y = jnp.concatenate([even[:, :, lanes], odd[:, :, lanes]], axis=2)
-                ladder[:, pl.ds(pl.multiple_of(128 * g + 32 * n, 32), 32), :] = y
+            low = lax.broadcasted_iota(jnp.int32, (32, 32, 128), 2) < 64
+            for n in range(2):
+                x0, x1 = even[:, :, 128 * n:128 * n + 128], odd[:, :, 128 * n:128 * n + 128]
+                mixed = jnp.where(low, x1, x0)
+                mixed = jnp.concatenate([mixed[:, :, 64:], mixed[:, :, :64]], axis=2)
+                at_b = pl.multiple_of(128 * g + 64 * n, 64)
+                ladder[:, pl.ds(at_b, 32), :] = jnp.where(low, x0, mixed)
+                ladder[:, pl.ds(at_b + 32, 32), :] = jnp.where(low, mixed, x1)
             return 0
 
         lax.fori_loop(0, 2 * pairs, body, 0)

time: 88.4 us -> 87.9 us (level)
  no operation moved by 1% of the time
where the time goes in v4:
time: 87.9 us; the launch traced here: 87.6 us
  Pallas kernels  83.3 us (95%)
  other arithmetic  3.44 us (4%)
    pallas_call x1, Pallas kernels, on_device(): pl.pallas_call(ladder_kernel, out_shape=jax.ShapeDtypeStruct((16, 1024),...  83.3 us
    reduce_sum x3, other arithmetic, select_energy(): jnp.sum(jnp.where(positions[:, None] == labels[None, :], table[None, :],...  1.86 us

profile of v4, /device:TPU:0, one launch (start us, length us, event | category | flops | bytes accessed | tf_op | source)
XLA Modules:
  0.0 87.6 jit_solution(8795048628940017513)
XLA Ops:
  0.0 0.9 select_reduce_fusion.2
  0.9 0.2 select_reduce_fusion.3
  1.1 0.8 fusion
  1.9 0.8 select_reduce_fusion
  2.7 83.3 %shard_map.73 = f32[16,1024]{1,0:T(8,128)} custom-call(bf16[2048,128]{1,0:T(8,128)(2,1)} %bitcast.9, bf16[128,1024]{1,0:T(8,128)(2,1)} %met.1, bf16[4096,1024]{1,0:T(8,128)(2,1)} %bitcast.8), custom_call_target="tpu_custom_call" | custom-call | flops 25999998976 | bytes 10000000 | tf_op jit(solution)/shard_map/pallas_call | solution.py:340
  86.0 1.6 %subtract_divide_fusion = f32[16,1024]{1,0:T(8,128)} fusion(f32[16,1024]{1,0:T(8,128)} %shard_map.73, f32[16]{0:T(128)S(1)} %add.50, f32[1024]{0:T(1024)S(1)} %add.45), kind=kLoop, calls=%fused_computation.4 | loop fusion | flops 32768 | bytes 135232 | tf_op jit(solution)/shard_map/div | solution.py:376
  (3 shorter events, 0.0 us)
